TPU v7x, 32 devices: a whole 2x2x4 slice. The times are simulated.
32 devices in a mesh: gx: 16 (over z, x, core), gy: 2 (over y).
Axes of the slice: x: 2, y: 2, z: 4, core: 2. Of those that a mesh axis runs over, the one named last changes fastest.
Arguments:
- populations: float32 [19, 16, 256, 256], P(None, None, 'gx', 'gy'), as said below
- solid_mask: int32 [16, 256, 256], P(None, 'gx', 'gy'), may hold values 0 or 1
- bead_states: float32 [16, 2, 8, 9, 1280], P('gx', 'gy'), as said below
- bead_bricks: int32 [16, 2, 8, 20], P('gx', 'gy'), may hold values from 0 to 63, as said below
- leave_dir: int32 [16, 2, 8], P('gx', 'gy'), may hold values from 0 to 4, as said below
- stiffness: bfloat16 [1280, 1280], replicated, may hold values from -0.15625 to 0.15625
Outputs:
- populations_out: float32 [19, 16, 256, 256], P(None, None, 'gx', 'gy')
- vertex_out: float32 [16, 2, 16, 9, 1280], P('gx', 'gy')
Inputs may be any that keep to these rules, and one draw needn't show every extreme that they name: `populations`: every entry is positive. `bead_states`: in the second dimension from the end, entries 0 to 2 are a vertex's x, y, z cell coordinates inside its block's brick, from 1 to 6; entries 3 to 5 its displacement from the reference shape; entries 6 to 8 its velocity. Every slot holds a bead. `bead_bricks`: a brick index counted in the tile that holds the bead after migration. `leave_dir`: 0 keeps the bead on its tile; 1 and 2 move it to the next tile along +x and -x, 3 and 4 along +y and -y. On every tile at most 2 beads have any one code from 1 to 4, and exactly 2 have one of them.
All inputs are finite; a program needn't handle non-finite values. No bound on the sum of `solid_mask` on one device may be relied on, other than what follows from the above.
Results may differ from a plain program's by a relative error of at most 0.00036.
Values sent between devices are 32-bit elements; how exact they have to be, the bound alone decides.
A program may use at most 128 MiB of HBM per device.

v0:
```python
import functools

import jax
import jax.numpy as jnp
import numpy as np
from jax import lax
from jax.experimental import pallas as pl
from jax.experimental.pallas import tpu as pltpu
from jax.sharding import PartitionSpec as P

MIG = 2
LATTICE = [
    (0, 0, 0),
    (1, 0, 0), (-1, 0, 0),
    (0, 1, 0), (0, -1, 0),
    (0, 0, 1), (0, 0, -1),
    (1, 1, 0), (-1, -1, 0),
    (1, -1, 0), (-1, 1, 0),
    (1, 0, 1), (-1, 0, -1),
    (1, 0, -1), (-1, 0, 1),
    (0, 1, 1), (0, -1, -1),
    (0, 1, -1), (0, -1, 1),
]
WEIGHTS = [1.0 / 3.0] + [1.0 / 18.0] * 6 + [1.0 / 36.0] * 12
X_UP = [q for q in range(19) if LATTICE[q][0] == 1]
X_DOWN = [q for q in range(19) if LATTICE[q][0] == -1]
Y_UP = [q for q in range(19) if LATTICE[q][1] == 1]
Y_DOWN = [q for q in range(19) if LATTICE[q][1] == -1]
MESH = pl.DeviceIdType.MESH
COS_FIT = [
    float(c)
    for c in np.polynomial.Chebyshev.interpolate(
        lambda u: np.cos(np.pi * np.sqrt(np.maximum(u, 0.0)) / 4.0), 5, domain=[0.0, 4.0]
    ).convert(kind=np.polynomial.Polynomial).coef
]


def exchange_kernel(
    sizes,
    leave_hbm,
    bricks_hbm,
    states_hbm,
    pops_hbm,
    beads_ref,
    read_hbm,
    moment_hbm,
    velocity_hbm,
    read_ref,
    moment_ref,
    velocity_ref,
    leave_ref,
    bricks_ref,
    states_ref,
    pops_ref,
    bead_out,
    x_out,
    y_out,
    xface_ref,
    yface_ref,
    corner_ref,
    diagonal_ref,
    field_ref,
    load_sems,
    store_sems,
    send_sems,
    recv_sems,
):
    n_gx, n_gy = sizes
    f32 = jnp.float32
    loads = [
        pltpu.make_async_copy(src, dst, load_sems.at[i])
        for i, (src, dst) in enumerate(
            (
                (leave_hbm, leave_ref),
                (bricks_hbm, bricks_ref),
                (states_hbm, states_ref),
                (pops_hbm, pops_ref),
            )
        )
    ]
    for load in loads:
        load.start()
    depth, width = pops_ref.shape[1], pops_ref.shape[2]
    slots = states_ref.shape[1]
    tiles = states_ref.shape[2] // 128
    blocks = bricks_ref.shape[1]
    bx_count, by_count = width // 8, 16
    ax, ay = lax.axis_index("gx"), lax.axis_index("gy")
    xp, xm = lax.rem(ax + 1, n_gx), lax.rem(ax + n_gx - 1, n_gx)
    yp, ym = lax.rem(ay + 1, n_gy), lax.rem(ay + n_gy - 1, n_gy)
    barrier = pltpu.get_barrier_semaphore()
    for where in ((xp, ay), (xm, ay), (ax, yp), (ax, ym), (xp, yp), (xm, ym), (xp, ym), (xm, yp)):
        pl.semaphore_signal(barrier, inc=1, device_id=where, device_id_type=MESH)

    for load in loads[:3]:
        load.wait()
    leaving = [leave_ref[0, s] for s in range(slots)]
    last = MIG * tiles * 8
    row = MIG * tiles * 9
    for d in (2, 3, 0, 1):
        first, second, count = jnp.int32(0), jnp.int32(0), jnp.int32(0)
        for s in range(slots):
            hit = leaving[s] == d + 1
            first = jnp.where(hit & (count == 0), s, first)
            second = jnp.where(hit & (count == 1), s, second)
            count = count + jnp.where(hit, 1, 0)
        for m, at in enumerate((first, second)):
            for c in range(9):
                line = states_ref[c, pl.ds(at, 1), :]
                for j in range(tiles):
                    to = j * 16 + 2 * c + m if c < 8 else last + 2 * j + m
                    bead_out[d, to : to + 1, :] = line[:, j * 128 : (j + 1) * 128]
            valid = jnp.where(count > m, 1.0, 0.0).astype(f32)
            bead_out[d, row + m : row + m + 1, :] = jnp.full((1, 128), valid, f32)
            bead_out[d, row + m : row + m + 1, 0:blocks] = bricks_ref[pl.ds(at, 1), :].astype(f32)

    loads[3].wait()
    for i, q in enumerate(X_UP):
        x_out[0, i] = pops_ref[q, :, width - 1, :]
    for i, q in enumerate(X_DOWN):
        x_out[1, i] = pops_ref[q, :, 0, :]
    lane = lax.broadcasted_iota(jnp.int32, (width, 128), 1)
    for side, (group, edge) in enumerate(((Y_UP, 127), (Y_DOWN, 0))):
        packed = jnp.zeros((width, 128), f32)
        for i, q in enumerate(group):
            for z in range(depth):
                t = i * depth + z
                packed = jnp.where(
                    lane == t, pltpu.roll(pops_ref[q, z], (t - edge) % 128, 1), packed
                )
        y_out[side] = packed

    pl.semaphore_wait(barrier, 8)
    copies = []

    def send(src, dst, where):
        at = len(copies)
        copy = pltpu.make_async_remote_copy(
            src_ref=src,
            dst_ref=dst,
            send_sem=send_sems.at[at],
            recv_sem=recv_sems.at[at],
            device_id=where,
            device_id_type=MESH,
        )
        copy.start()
        copies.append(copy)

    targets = ((xp, ay), (xm, ay), (ax, yp), (ax, ym))
    send(y_out.at[0], yface_ref.at[0], targets[2])
    send(y_out.at[1], yface_ref.at[1], targets[3])
    send(y_out.at[0, width - 8 : width], corner_ref.at[0], (xp, yp))
    send(y_out.at[1, 0:8], corner_ref.at[1], (xm, ym))
    send(y_out.at[1, width - 8 : width], corner_ref.at[2], (xp, ym))
    send(y_out.at[0, 0:8], corner_ref.at[3], (xm, yp))
    send(x_out.at[0], xface_ref.at[0], targets[0])
    send(x_out.at[1], xface_ref.at[1], targets[1])
    for d in (2, 3, 0, 1):
        send(bead_out.at[d], beads_ref.at[d], targets[d])
    for copy in copies[:8]:
        copy.wait_recv()

    row8 = lax.broadcasted_iota(jnp.int32, (width, 128), 0)
    for i, (side, up) in enumerate(((0, True), (1, False), (1, True), (0, False))):
        face = yface_ref[side]
        if up:
            edge = jnp.broadcast_to(corner_ref[i, 7:8, :], (width, 128))
            diagonal_ref[i] = jnp.where(row8 == 0, edge, pltpu.roll(face, 1, 0))
        else:
            edge = jnp.broadcast_to(corner_ref[i, 0:1, :], (width, 128))
            diagonal_ref[i] = jnp.where(row8 == width - 1, edge, pltpu.roll(face, width - 1, 0))

    def pull(z, carry):
        density = None
        sums = [None, None, None]
        for q in range(19):
            cx, cy, cz = LATTICE[q]
            zs = z if cz == 0 else lax.rem(z - cz + depth, depth)
            value = pops_ref[q, zs]
            if cx == 1:
                edge = xface_ref[0, X_UP.index(q), pl.ds(zs, 1), :]
                value = jnp.where(row8 == 0, edge, pltpu.roll(value, 1, 0))
            elif cx == -1:
                edge = xface_ref[1, X_DOWN.index(q), pl.ds(zs, 1), :]
                value = jnp.where(row8 == width - 1, edge, pltpu.roll(value, width - 1, 0))
            if cy != 0:
                face = diagonal_ref[q - 7] if cx != 0 else yface_ref[0 if cy == 1 else 1]
                t = (Y_UP if cy == 1 else Y_DOWN).index(q) * depth + zs
                if cy == 1:
                    edge = pltpu.roll(face, lax.rem(128 - t, 128), 1)
                    value = jnp.where(lane == 0, edge, pltpu.roll(value, 1, 1))
                else:
                    edge = pltpu.roll(face, 127 - t, 1)
                    value = jnp.where(lane == 127, edge, pltpu.roll(value, 127, 1))
            read_ref[q, z] = value
            density = value if density is None else density + value
            for axis, c in enumerate((cx, cy, cz)):
                if c == 1:
                    sums[axis] = value if sums[axis] is None else sums[axis] + value
                elif c == -1:
                    sums[axis] = sums[axis] - value
        inverse = 1.0 / density
        moment_ref[0, z] = density
        moment_ref[4, z] = inverse
        for axis in range(3):
            moment_ref[1 + axis, z] = sums[axis]
            field_ref[axis, z] = (sums[axis] * inverse).astype(jnp.bfloat16).astype(f32)
        pltpu.make_async_copy(read_ref.at[:, z], read_hbm.at[:, z], store_sems.at[z]).start()
        return carry

    lax.fori_loop(0, depth, pull, 0)
    stored = pltpu.make_async_copy(moment_ref, moment_hbm, store_sems.at[depth])
    stored.start()

    for axis in range(3):
        for bz in range(depth // 8):
            cells = jnp.concatenate(
                [
                    field_ref[axis, bz * 8 + iz, bx * 8 : bx * 8 + 8, :]
                    for bx in range(bx_count)
                    for iz in range(8)
                ],
                axis=0,
            )
            turned = cells.T
            for bx in range(bx_count):
                laid = turned if bx == 0 else pltpu.roll(turned, 64, 1)
                for by in range(by_count):
                    brick = (bz * bx_count + bx) * by_count + by
                    velocity_ref[brick, axis * 8 : axis * 8 + 8, :] = laid[by * 8 : by * 8 + 8, :]

    laid_out = pltpu.make_async_copy(velocity_ref, velocity_hbm, store_sems.at[depth + 1])
    laid_out.start()

    def finish(z, carry):
        pltpu.make_async_copy(read_ref.at[:, z], read_hbm.at[:, z], store_sems.at[z]).wait()
        return carry

    lax.fori_loop(0, depth, finish, 0)
    stored.wait()
    for copy in copies[:8]:
        copy.wait_send()
    for copy in copies[8:]:
        copy.wait()
    laid_out.wait()


def exchange(populations, states, bricks, leaving, sizes):
    depth, width = populations.shape[1], populations.shape[2]
    tiles = states.shape[2] // 128
    rows = -(-MIG * (tiles * 9 + 1) // 8) * 8
    n_bricks = (depth // 8) * (width // 8) * 16
    hbm = pl.BlockSpec(memory_space=pltpu.HBM)
    f32 = jnp.float32
    return pl.pallas_call(
        functools.partial(exchange_kernel, sizes),
        out_shape=(
            jax.ShapeDtypeStruct((4, rows, 128), f32),
            jax.ShapeDtypeStruct(populations.shape, f32),
            jax.ShapeDtypeStruct((5, depth, width, 128), f32),
            jax.ShapeDtypeStruct((n_bricks, 24, 128), f32),
        ),
        in_specs=[hbm] * 4,
        out_specs=(hbm,) * 4,
        scratch_shapes=[
            pltpu.VMEM(populations.shape, f32),
            pltpu.VMEM((5, depth, width, 128), f32),
            pltpu.VMEM((n_bricks, 24, 128), f32),
            pltpu.SMEM(leaving.shape, jnp.int32),
            pltpu.VMEM(bricks.shape, jnp.int32),
            pltpu.VMEM(states.shape, f32),
            pltpu.VMEM(populations.shape, f32),
            pltpu.VMEM((4, rows, 128), f32),
            pltpu.VMEM((2, 5, depth, 128), f32),
            pltpu.VMEM((2, width, 128), f32),
            pltpu.VMEM((2, 5, depth, 128), f32),
            pltpu.VMEM((2, width, 128), f32),
            pltpu.VMEM((4, 8, 128), f32),
            pltpu.VMEM((4, width, 128), f32),
            pltpu.VMEM((3, depth, width, 128), f32),
            pltpu.SemaphoreType.DMA((4,)),
            pltpu.SemaphoreType.DMA((depth + 2,)),
            pltpu.SemaphoreType.DMA((12,)),
            pltpu.SemaphoreType.DMA((12,)),
        ],
        compiler_params=pltpu.CompilerParams(
            collective_id=0, has_side_effects=True, vmem_limit_bytes=56 * 1024 * 1024
        ),
        name="exchange",
    )(leaving, bricks, states, populations)


def phi(distance):
    square = distance * distance
    u = jnp.minimum(square, 4.0)
    value = jnp.full_like(u, COS_FIT[5])
    for c in COS_FIT[4::-1]:
        value = value * u + c
    return jnp.where(square < 4.0, 0.5 * value * value, 0.0)


def step_kernel(
    leave_hbm,
    bricks_hbm,
    states_hbm,
    beads_hbm,
    solid_hbm,
    read_hbm,
    moment_hbm,
    velocity_hbm,
    stiff_hbm,
    pops_out,
    vertex_out,
    leave_ref,
    bricks_ref,
    meta_ref,
    states_ref,
    beads_ref,
    solid_ref,
    read_ref,
    moment_ref,
    velocity_ref,
    stiff_ref,
    fresh_ref,
    field_ref,
    force_ref,
    moved_ref,
    node_ref,
    sampled_ref,
    vertex_ref,
    weight_ref,
    slot_ref,
    sems,
    load_sems,
):
    meta_at = beads_hbm.shape[1] - 8
    pairs = [(leave_hbm, leave_ref), (bricks_hbm, bricks_ref)]
    pairs += [(beads_hbm.at[d, meta_at : meta_at + 8], meta_ref.at[d]) for d in range(4)]
    pairs += [(states_hbm, states_ref), (beads_hbm, beads_ref), (stiff_hbm, stiff_ref)]
    pairs += [(velocity_hbm, velocity_ref)]
    pairs += [(read_hbm, read_ref), (moment_hbm, moment_ref), (solid_hbm, solid_ref)]
    loads = [
        pltpu.make_async_copy(src, dst, load_sems.at[i]) for i, (src, dst) in enumerate(pairs)
    ]
    for load in loads:
        load.start()
    depth, width = read_ref.shape[1], read_ref.shape[2]
    slots = states_ref.shape[1]
    vertices = states_ref.shape[2]
    tiles = vertices // 128
    quads = vertices // 256
    bx_count, by_count = width // 8, 16
    total = slots + 4 * MIG
    f32 = jnp.float32

    force_ref[...] = jnp.zeros_like(force_ref)
    for load in loads[:8]:
        load.wait()
    meta_row = MIG * tiles * 9 - meta_at
    last = MIG * tiles * 8
    for c in range(9):
        moved_ref[c, 0:slots, :] = states_ref[c]
        for j in range(tiles):
            at = j * 16 + 2 * c if c < 8 else last + 2 * j
            moved_ref[c, slots:total, j * 128 : (j + 1) * 128] = jnp.concatenate(
                [beads_ref[d, at : at + MIG, :] for d in range(4)], axis=0
            )
    count = jnp.int32(0)
    blocks = bricks_ref.shape[1]
    row16 = lax.broadcasted_iota(jnp.int32, (total, 128), 0)
    active = jnp.zeros((total, 128), jnp.int32)
    for s in range(total):
        slot_ref[count] = s
        if s < slots:
            here = jnp.where(leave_ref[0, s] == 0, 1, 0)
        else:
            d, m = divmod(s - slots, MIG)
            here = jnp.where(meta_ref[d, meta_row + m, blocks] > 0.5, 1, 0)
        count = count + here
        active = jnp.where(row16 == s, here, active)

    rows = moved_ref[3:6].reshape(3 * total, vertices).astype(jnp.bfloat16)
    loads[8].wait()
    for g in range(quads):
        part = jnp.dot(
            rows, stiff_ref[:, g * 256 : (g + 1) * 256], preferred_element_type=f32
        )
        node_ref[:, g * 256 : (g + 1) * 256] = -part

    loads[9].wait()
    sampled_ref[...] = jnp.zeros_like(sampled_ref)
    lane8 = lax.broadcasted_iota(jnp.int32, (8, 128), 1)
    row8 = lax.broadcasted_iota(jnp.int32, (8, 256), 0)
    steps8 = row8.astype(f32)
    group = lax.broadcasted_iota(jnp.int32, (8, 256), 1) // 64

    def couple(i, carry):
        s = slot_ref[i]
        own = s < slots
        inside = jnp.minimum(s, slots - 1)
        outside = jnp.maximum(s - slots, 0)
        for g in range(quads):
            cols = slice(g * 256, (g + 1) * 256)
            where = [
                jnp.where(
                    own,
                    bricks_ref[inside, 4 * g + j],
                    meta_ref[
                        outside // MIG, meta_row + outside % MIG, 4 * g + j
                    ].astype(jnp.int32),
                )
                for j in range(4)
            ]
            along_x = phi(moved_ref[0, pl.ds(s, 1), cols] - steps8)
            along_y = phi(moved_ref[1, pl.ds(s, 1), cols] - steps8)
            along_z = phi(moved_ref[2, pl.ds(s, 1), cols] - steps8)
            zx = [along_z[iz : iz + 1, :] * along_x for iz in range(8)]
            for k in range(4):
                for h in range(2):
                    iy = k + 4 * h
                    y_row = jnp.broadcast_to(along_y[iy : iy + 1, :], (8, 256))
                    for iz in range(0, 8, 2):
                        pair = jnp.concatenate([zx[iz] * y_row, zx[iz + 1] * y_row], axis=0)
                        at = (k * 2 + h) * 64 + iz * 8
                        weight_ref[g, at : at + 16, :] = pair.astype(jnp.bfloat16)
            near = jnp.concatenate([velocity_ref[r] for r in where], axis=0)
            flat = jnp.concatenate(zx, axis=0).astype(jnp.bfloat16)
            sampled = jnp.dot(
                near[:, 0:64].astype(jnp.bfloat16), flat, preferred_element_type=f32
            )
            for c in range(3):
                vertex = sampled[8 * c : 8 * c + 8, :]
                for j in range(1, 4):
                    at = 24 * j + 8 * c
                    vertex = jnp.where(group == j, sampled[at : at + 8, :], vertex)
                sampled_ref[c, pl.ds(s, 1), cols] = jnp.sum(
                    vertex * along_y, axis=0, keepdims=True
                )
            force = jnp.zeros((8, 256), f32)
            for c in range(3):
                force = jnp.where(row8 == c, node_ref[pl.ds(c * total + s, 1), cols], force)
            spreading = jnp.concatenate(
                [jnp.where(group == j, force, 0.0) for j in range(4)], axis=0
            ).astype(jnp.bfloat16)
            spread = lax.dot_general(
                spreading, weight_ref[g], (((1,), (1,)), ((), ())), preferred_element_type=f32
            )
            for j in range(4):
                for k in range(4):
                    force_ref[where[j], k] = (
                        force_ref[where[j], k]
                        + spread[8 * j : 8 * j + 8, k * 128 : (k + 1) * 128]
                    )
        return carry

    lax.fori_loop(0, count, couple, 0)

    for j in range(tiles):
        cols = slice(j * 128, (j + 1) * 128)
        for c in range(3):
            speed = sampled_ref[c, :, cols]
            half = 0.5 * (moved_ref[6 + c, :, cols] + speed)
            vertex_ref[c, :, cols] = jnp.where(active > 0, moved_ref[c, :, cols] + half, 0.0)
            vertex_ref[3 + c, :, cols] = jnp.where(
                active > 0, moved_ref[3 + c, :, cols] + half, 0.0
            )
            vertex_ref[6 + c, :, cols] = speed
    finished = pltpu.make_async_copy(vertex_ref, vertex_out, sems.at[depth])
    finished.start()

    for load in loads[10:]:
        load.wait()
    for axis in range(3):
        for bz in range(depth // 8):
            parts = []
            for by in range(by_count):
                laid = []
                for bx in range(bx_count):
                    brick = (bz * bx_count + bx) * by_count + by
                    got = [force_ref[brick, k, axis : axis + 1, :] for k in range(4)]
                    laid.append(jnp.concatenate(got + got, axis=0))
                top = lax.broadcasted_iota(jnp.int32, (8, 128), 0) < 4
                low = jnp.where(top, laid[0], pltpu.roll(laid[0], 64, 1))
                high = jnp.where(top, pltpu.roll(laid[1], 64, 1), laid[1])
                parts.append(jnp.where(lane8 < 64, low, high))
            cells = jnp.concatenate(parts, axis=0).T
            for bx in range(bx_count):
                for iz in range(8):
                    at = (bx * 8 + iz) * 8
                    field_ref[axis, bz * 8 + iz, bx * 8 : bx * 8 + 8, :] = cells[at : at + 8, :]

    def collide(z, carry):
        density, inverse = moment_ref[0, z], moment_ref[4, z]
        force = [field_ref[axis, z] for axis in range(3)]
        speed = [(moment_ref[1 + axis, z] + 0.5 * force[axis]) * inverse for axis in range(3)]
        square = speed[0] * speed[0] + speed[1] * speed[1] + speed[2] * speed[2]
        dot = speed[0] * force[0] + speed[1] * force[1] + speed[2] * force[2]
        fluid = solid_ref[z] == 0
        base = (1.25 * density) * (1.0 - 1.5 * square) - 1.125 * dot
        dense = 5.625 * density
        odd = [3.75 * density * speed[axis] + 1.125 * force[axis] for axis in range(3)]
        slope = [3.375 * force[axis] for axis in range(3)]
        rest = read_ref[0, z]
        fresh_ref[0, z] = jnp.where(fluid, WEIGHTS[0] * base - 0.25 * rest, rest)

        def along(vector, c):
            terms = None
            for axis in range(3):
                if c[axis] == 0:
                    continue
                if terms is None:
                    terms = vector[axis] if c[axis] == 1 else -vector[axis]
                else:
                    terms = terms + vector[axis] if c[axis] == 1 else terms - vector[axis]
            return terms

        for q in range(1, 19, 2):
            c = LATTICE[q]
            e = along(speed, c)
            even = WEIGHTS[q] * (base + e * (dense * e + along(slope, c)))
            skew = WEIGHTS[q] * along(odd, c)
            ahead, back = read_ref[q, z], read_ref[q + 1, z]
            fresh_ref[q, z] = jnp.where(fluid, even + skew - 0.25 * ahead, back)
            fresh_ref[q + 1, z] = jnp.where(fluid, even - skew - 0.25 * back, ahead)
        pltpu.make_async_copy(fresh_ref.at[:, z], pops_out.at[:, z], sems.at[z]).start()
        return carry

    lax.fori_loop(0, depth, collide, 0)

    def finish(z, carry):
        pltpu.make_async_copy(fresh_ref.at[:, z], pops_out.at[:, z], sems.at[z]).wait()
        return carry

    lax.fori_loop(0, depth, finish, 0)
    finished.wait()


def advance(leaving, bricks, states, beads, solid, read, moment, velocity, stiffness):
    depth, width = read.shape[1], read.shape[2]
    slots, vertices = states.shape[1], states.shape[2]
    total = slots + 4 * MIG
    n_bricks = velocity.shape[0]
    hbm = pl.BlockSpec(memory_space=pltpu.HBM)
    f32 = jnp.float32
    return pl.pallas_call(
        step_kernel,
        out_shape=(
            jax.ShapeDtypeStruct(read.shape, f32),
            jax.ShapeDtypeStruct((9, total, vertices), f32),
        ),
        in_specs=[hbm] * 9,
        out_specs=(hbm, hbm),
        scratch_shapes=[
            pltpu.SMEM(leaving.shape, jnp.int32),
            pltpu.SMEM(bricks.shape, jnp.int32),
            pltpu.SMEM((4, 8, 128), f32),
            pltpu.VMEM(states.shape, f32),
            pltpu.VMEM(beads.shape, f32),
            pltpu.VMEM(solid.shape, jnp.int32),
            pltpu.VMEM(read.shape, f32),
            pltpu.VMEM(moment.shape, f32),
            pltpu.VMEM(velocity.shape, f32),
            pltpu.VMEM(stiffness.shape, stiffness.dtype),
            pltpu.VMEM(read.shape, f32),
            pltpu.VMEM((3, depth, width, 128), f32),
            pltpu.VMEM((n_bricks, 4, 8, 128), f32),
            pltpu.VMEM((9, total, vertices), f32),
            pltpu.VMEM((total * 3, vertices), f32),
            pltpu.VMEM((3, total, vertices), f32),
            pltpu.VMEM((9, total, vertices), f32),
            pltpu.VMEM((vertices // 256, 512, 256), jnp.bfloat16),
            pltpu.SMEM((total + 1,), jnp.int32),
            pltpu.SemaphoreType.DMA((depth + 1,)),
            pltpu.SemaphoreType.DMA((13,)),
        ],
        compiler_params=pltpu.CompilerParams(vmem_limit_bytes=56 * 1024 * 1024),
        name="step",
    )(leaving, bricks, states, beads, solid, read, moment, velocity, stiffness)


def solution(mesh):
    sizes = (mesh.shape["gx"], mesh.shape["gy"])

    def local(populations, solid_mask, bead_states, bead_bricks, leave_dir, stiffness):
        states = bead_states.reshape(bead_states.shape[2:]).transpose(1, 0, 2)
        bricks = bead_bricks.reshape(bead_bricks.shape[2:])
        leaving = leave_dir.reshape((1,) + leave_dir.shape[2:])
        beads, read, moment, velocity = exchange(
            populations, states, bricks, leaving, sizes
        )
        populations_out, vertex_out = advance(
            leaving, bricks, states, beads, solid_mask, read, moment, velocity, stiffness
        )
        vertex_out = vertex_out.transpose(1, 0, 2)
        return (populations_out, vertex_out.reshape((1, 1) + vertex_out.shape))

    return jax.shard_map(
        local,
        mesh=mesh,
        in_specs=(
            P(None, None, "gx", "gy"),
            P(None, "gx", "gy"),
            P("gx", "gy", None, None, None),
            P("gx", "gy", None, None),
            P("gx", "gy", None),
            P(),
        ),
        out_specs=(P(None, None, "gx", "gy"), P("gx", "gy", None, None, None)),
        check_vma=False,
    )
```

profile of v0, /device:TPU:1, one launch (start us, length us, event | category | flops | bytes accessed | tf_op | source)
XLA Modules:
  0.0 24.4 jit_solution(3415844842738753760)
XLA Ops:
  0.6 12.1 %exchange.1 = (f32[4,184,128]{2,1,0:T(8,128)}, f32[19,16,16,128]{3,2,1,0:T(8,128)}, f32[5,16,16,128]{3,2,1,0:T(8,128)}, f32[64,24,128]{2,1,0:T(8,128)}) custom-call(s32[1,8]{1,0:T(1,128)} %bitcast.12, s32[8,20]{1,0:T(8,128)} %bitcast.10, f32[9,8,1280]{2,1,0:T(8,128)} %bitcast.8, f32[19,16,16,128]{3,2,1,0:T(8,128)} %pops_hbm.1), custom_call_target="tpu_custom_call" | custom-call | tf_op jit(solution)/shard_map/exchange/pallas_call | solution.py:255
  12.7 11.6 %step.1 = (f32[19,16,16,128]{3,2,1,0:T(8,128)}, f32[9,16,1280]{2,1,0:T(8,128)}) custom-call(s32[1,8]{1,0:T(1,128)} %bitcast.13, s32[8,20]{1,0:T(8,128)} %bitcast.11, f32[9,8,1280]{2,1,0:T(8,128)} %bitcast.9, f32[4,184,128]{2,1,0:T(8,128)} %get-tuple-element.8.beads_hbm, s32[16,16,128]{2,1,0:T(8,128)} %solid_hbm.1, ...), custom_call_target="tpu_custom_call" | custom-call | tf_op jit(solution)/shard_map/step/pallas_call | solution.py:545
where the time goes:
time: 24.2 us; the launch traced here: 24.4 us
  Pallas kernels  23.7 us (98%)
  between operations  0.64 us (3%)
    pallas_call x1, Pallas kernels, exchange(): pl.pallas_call(functools.partial(exchange_kernel, sizes), out_shape=(jax....  12.1 us
    pallas_call x1, Pallas kernels, advance(): pl.pallas_call(step_kernel, out_shape=(jax.ShapeDtypeStruct(read.shape, f...  11.6 us

commit v1 on v0

--- a/solution.py
+++ b/solution.py
@@ -95,9 +95,26 @@
     for load in loads[:3]:
         load.wait()
     leaving = [leave_ref[0, s] for s in range(slots)]
+    copies = []
+
+    def send(src, dst, where):
+        at = len(copies)
+        copy = pltpu.make_async_remote_copy(
+            src_ref=src,
+            dst_ref=dst,
+            send_sem=send_sems.at[at],
+            recv_sem=recv_sems.at[at],
+            device_id=where,
+            device_id_type=MESH,
+        )
+        copy.start()
+        copies.append(copy)
+        return copy
+
+    targets = ((xp, ay), (xm, ay), (ax, yp), (ax, ym))
     last = MIG * tiles * 8
     row = MIG * tiles * 9
-    for d in (2, 3, 0, 1):
+    for d in (2, 0, 3, 1):
         first, second, count = jnp.int32(0), jnp.int32(0), jnp.int32(0)
         for s in range(slots):
             hit = leaving[s] == d + 1
@@ -113,6 +130,10 @@
             valid = jnp.where(count > m, 1.0, 0.0).astype(f32)
             bead_out[d, row + m : row + m + 1, :] = jnp.full((1, 128), valid, f32)
             bead_out[d, row + m : row + m + 1, 0:blocks] = bricks_ref[pl.ds(at, 1), :].astype(f32)
+        if d == 2:
+            pl.semaphore_wait(barrier, 8)
+        if d in (2, 0):
+            send(bead_out.at[d], beads_ref.at[d], targets[d])
 
     loads[3].wait()
     for i, q in enumerate(X_UP):
@@ -130,34 +151,19 @@
                 )
         y_out[side] = packed
 
-    pl.semaphore_wait(barrier, 8)
-    copies = []
-
-    def send(src, dst, where):
-        at = len(copies)
-        copy = pltpu.make_async_remote_copy(
-            src_ref=src,
-            dst_ref=dst,
-            send_sem=send_sems.at[at],
-            recv_sem=recv_sems.at[at],
-            device_id=where,
-            device_id_type=MESH,
-        )
-        copy.start()
-        copies.append(copy)
-
-    targets = ((xp, ay), (xm, ay), (ax, yp), (ax, ym))
-    send(y_out.at[0], yface_ref.at[0], targets[2])
-    send(y_out.at[1], yface_ref.at[1], targets[3])
-    send(y_out.at[0, width - 8 : width], corner_ref.at[0], (xp, yp))
-    send(y_out.at[1, 0:8], corner_ref.at[1], (xm, ym))
-    send(y_out.at[1, width - 8 : width], corner_ref.at[2], (xp, ym))
-    send(y_out.at[0, 0:8], corner_ref.at[3], (xm, yp))
-    send(x_out.at[0], xface_ref.at[0], targets[0])
-    send(x_out.at[1], xface_ref.at[1], targets[1])
-    for d in (2, 3, 0, 1):
+    faces = [
+        send(y_out.at[0], yface_ref.at[0], targets[2]),
+        send(y_out.at[1], yface_ref.at[1], targets[3]),
+        send(y_out.at[0, width - 8 : width], corner_ref.at[0], (xp, yp)),
+        send(y_out.at[1, 0:8], corner_ref.at[1], (xm, ym)),
+        send(y_out.at[1, width - 8 : width], corner_ref.at[2], (xp, ym)),
+        send(y_out.at[0, 0:8], corner_ref.at[3], (xm, yp)),
+        send(x_out.at[0], xface_ref.at[0], targets[0]),
+        send(x_out.at[1], xface_ref.at[1], targets[1]),
+    ]
+    for d in (3, 1):
         send(bead_out.at[d], beads_ref.at[d], targets[d])
-    for copy in copies[:8]:
+    for copy in faces:
         copy.wait_recv()
 
     row8 = lax.broadcasted_iota(jnp.int32, (width, 128), 0)
@@ -238,10 +244,11 @@
 
     lax.fori_loop(0, depth, finish, 0)
     stored.wait()
-    for copy in copies[:8]:
+    for copy in copies:
         copy.wait_send()
-    for copy in copies[8:]:
-        copy.wait()
+    for copy in copies:
+        if not any(copy is face for face in faces):
+            copy.wait_recv()
     laid_out.wait()
 
 
@@ -336,7 +343,11 @@
     meta_at = beads_hbm.shape[1] - 8
     pairs = [(leave_hbm, leave_ref), (bricks_hbm, bricks_ref)]
     pairs += [(beads_hbm.at[d, meta_at : meta_at + 8], meta_ref.at[d]) for d in range(4)]
-    pairs += [(states_hbm, states_ref), (beads_hbm, beads_ref), (stiff_hbm, stiff_ref)]
+    pairs += [(states_hbm, states_ref), (beads_hbm, beads_ref)]
+    parts = stiff_hbm.shape[1] // 256
+    for g in range(parts):
+        cols = slice(g * 256, (g + 1) * 256)
+        pairs += [(stiff_hbm.at[:, cols], stiff_ref.at[:, cols])]
     pairs += [(velocity_hbm, velocity_ref)]
     pairs += [(read_hbm, read_ref), (moment_hbm, moment_ref), (solid_hbm, solid_ref)]
     loads = [
@@ -380,14 +391,14 @@
         active = jnp.where(row16 == s, here, active)
 
     rows = moved_ref[3:6].reshape(3 * total, vertices).astype(jnp.bfloat16)
-    loads[8].wait()
     for g in range(quads):
+        loads[8 + g].wait()
         part = jnp.dot(
             rows, stiff_ref[:, g * 256 : (g + 1) * 256], preferred_element_type=f32
         )
         node_ref[:, g * 256 : (g + 1) * 256] = -part
 
-    loads[9].wait()
+    loads[8 + parts].wait()
     sampled_ref[...] = jnp.zeros_like(sampled_ref)
     lane8 = lax.broadcasted_iota(jnp.int32, (8, 128), 1)
     row8 = lax.broadcasted_iota(jnp.int32, (8, 256), 0)
@@ -468,7 +479,7 @@
     finished = pltpu.make_async_copy(vertex_ref, vertex_out, sems.at[depth])
     finished.start()
 
-    for load in loads[10:]:
+    for load in loads[9 + parts :]:
         load.wait()
     for axis in range(3):
         for bz in range(depth // 8):
@@ -525,7 +536,7 @@
         pltpu.make_async_copy(fresh_ref.at[:, z], pops_out.at[:, z], sems.at[z]).start()
         return carry
 
-    lax.fori_loop(0, depth, collide, 0)
+    lax.fori_loop(0, depth, collide, 0, unroll=2)
 
     def finish(z, carry):
         pltpu.make_async_copy(fresh_ref.at[:, z], pops_out.at[:, z], sems.at[z]).wait()
@@ -571,7 +582,7 @@
             pltpu.VMEM((vertices // 256, 512, 256), jnp.bfloat16),
             pltpu.SMEM((total + 1,), jnp.int32),
             pltpu.SemaphoreType.DMA((depth + 1,)),
-            pltpu.SemaphoreType.DMA((13,)),
+            pltpu.SemaphoreType.DMA((12 + vertices // 256,)),
         ],
         compiler_params=pltpu.CompilerParams(vmem_limit_bytes=56 * 1024 * 1024),
         name="step",

time: 24.2 us -> 25.1 us (1.037)
  Pallas kernels: 23.7 us -> 24.6 us
    pallas_call x1, Pallas kernels: 12.1 us -> 13.1 us  [exchange(): pl.pallas_call(functools.partial(exchange_kernel, sizes), out_shape=(jax....]
where the time goes in v1:
time: 25.1 us; the launch traced here: 25.2 us
  Pallas kernels  24.6 us (98%)
  between operations  0.64 us (3%)
    pallas_call x1, Pallas kernels, exchange(): pl.pallas_call(functools.partial(exchange_kernel, sizes), out_shape=(jax....  13.1 us
    pallas_call x1, Pallas kernels, advance(): pl.pallas_call(step_kernel, out_shape=(jax.ShapeDtypeStruct(read.shape, f...  11.5 us

profile of v1, /device:TPU:1, one launch (start us, length us, event | category | flops | bytes accessed | tf_op | source)
XLA Modules:
  0.0 25.2 jit_solution(10678407682672228166)
XLA Ops:
  0.6 13.1 %exchange.1 = (f32[4,184,128]{2,1,0:T(8,128)}, f32[19,16,16,128]{3,2,1,0:T(8,128)}, f32[5,16,16,128]{3,2,1,0:T(8,128)}, f32[64,24,128]{2,1,0:T(8,128)}) custom-call(s32[1,8]{1,0:T(1,128)} %bitcast.12, s32[8,20]{1,0:T(8,128)} %bitcast.10, f32[9,8,1280]{2,1,0:T(8,128)} %bitcast.8, f32[19,16,16,128]{3,2,1,0:T(8,128)} %pops_hbm.1), custom_call_target="tpu_custom_call" | custom-call | tf_op jit(solution)/shard_map/exchange/pallas_call | solution.py:262
  13.7 11.5 %step.1 = (f32[19,16,16,128]{3,2,1,0:T(8,128)}, f32[9,16,1280]{2,1,0:T(8,128)}) custom-call(s32[1,8]{1,0:T(1,128)} %bitcast.13, s32[8,20]{1,0:T(8,128)} %bitcast.11, f32[9,8,1280]{2,1,0:T(8,128)} %bitcast.9, f32[4,184,128]{2,1,0:T(8,128)} %get-tuple-element.8.beads_hbm, s32[16,16,128]{2,1,0:T(8,128)} %solid_hbm.1, ...), custom_call_target="tpu_custom_call" | custom-call | tf_op jit(solution)/shard_map/step/pallas_call | solution.py:556
